TPU v7x, 32 devices: a whole 2x2x4 slice. The times are simulated.
32 devices in a mesh: ens: 2 (over x), gx: 16 (over z, y, core).
Axes of the slice: x: 2, y: 2, z: 4, core: 2. Of those that a mesh axis runs over, the one named last changes fastest.
Arguments:
- state: float32 [2, 512, 32, 256], P(None, ('ens', 'gx')), parts along dimension 1, may hold values from -3 to 3
- fine_state: float32 [2, 64, 32, 1024], P(None, ('ens', 'gx')), parts along dimension 1, may hold values from -3 to 3
- box_list: int32 [64, 3], P('ens'), parts along dimension 0, may hold values from 0 to 240, as said below
- plan: int32 [64], P('ens'), parts along dimension 0, may hold values from 0 to 31, as said below
Outputs:
- coarse_out: float32 [2, 512, 32, 256], P(None, ('ens', 'gx')), parts along dimension 1
- fine_out: float32 [2, 64, 32, 1024], P(None, ('ens', 'gx')), parts along dimension 1
There are 2 independent parts, one for each index of `ens`. A program takes and returns all parts, laid end to end along the dimension named above; each array names one. Nothing has to cross between parts.
Inputs may be any that keep to these rules, and one draw needn't show every extreme that they name: `box_list`: every corner coordinate is a multiple of 16 within the grid; boxes do not intersect. plan is a permutation of the box numbers; the box in a slot of device d along gx (slot // 2 == d) has its x corner on device d or on device d - 1 cyclically (x corner // 16).
All inputs are finite; a program needn't handle non-finite values.
Results may differ from a plain program's by a relative error of at most 0.0003.
Values sent between devices are 32-bit elements; how exact they have to be, the bound alone decides.
A program may use at most 128 MiB of HBM per device.

v0:
```python
import jax
import jax.numpy as jnp
from jax import lax
from jax.experimental import pallas as pl
from jax.experimental.pallas import tpu as pltpu
from jax.sharding import PartitionSpec as P

FB = 32
BOX_DEV = 2
MESH = pl.DeviceIdType.MESH
BF = jnp.bfloat16
F32 = jnp.float32


def iota(shape, dim):
    return lax.broadcasted_iota(jnp.int32, shape, dim)


def halves(a):
    hi = a.astype(BF)
    lo = (a - hi.astype(F32)).astype(BF)
    return hi, lo


def mm(a, b):
    return jnp.dot(a, b, preferred_element_type=F32)


def mm_nt(a, b):
    return lax.dot_general(a, b, (((1,), (1,)), ((), ())), preferred_element_type=F32)


def star(d):
    d = jnp.abs(d)
    return jnp.where(d == 1, 16.0, jnp.where(d == 2, -1.0, 0.0))


def edge(side, j):
    d = jnp.where(side == 0, j, 31 - j)
    return jnp.where(d == 0, 15.0, jnp.where(d == 1, -1.0, 0.0))


def coarse_weights():
    k, j = iota((256, 256), 0), iota((256, 256), 1)
    d = (j - k) & 255
    d = jnp.minimum(d, 256 - d)
    return star(d).astype(BF)


def fine_weights():
    k, j = iota((256, 256), 0), iota((256, 256), 1)
    jy, jz = j >> 5, j & 31
    ky, kz = k >> 5, k & 31
    inner = jnp.where(ky == jy, star(kz - jz), 0.0) + jnp.where(kz == jz, star(ky - jy), 0.0)
    far = jnp.where(k < 128, ky - 4, ky + 4)
    outer = jnp.where(kz == jz, star(far - jy), 0.0)
    return inner.astype(BF), outer.astype(BF)


def boundary_weights():
    k, j = iota((128, 1024), 0), iota((128, 1024), 1)
    y, z = j >> 5, j & 31
    wy = jnp.where((k & 15) == (z >> 1), edge(k >> 6, y), 0.0).astype(BF)
    wzl = jnp.where((k & 31) == (y >> 1), edge(0, z), 0.0).astype(BF)
    wzh = jnp.where((k & 31) == (y >> 1), edge(1, z), 0.0).astype(BF)
    wx = jnp.where((k & 15) == (z >> 1), 1.0, 0.0).astype(BF)
    return wy, wzl, wzh, wx


def mean_weights():
    k, j = iota((1024, 256), 0), iota((1024, 256), 1)
    return jnp.where(((k >> 6) == (j >> 4)) & (((k & 31) >> 1) == (j & 15)), 1.0, 0.0).astype(BF)


def roll(a, shift, axis):
    return pltpu.roll(a, shift % a.shape[axis], axis)


def kernel(
    devices,
    state, fine, boxes, plan,
    coarse_out, fine_out,
    fe, pe, f2, f3, f4, k1, k2, nf, npm,
    q, pad, faces, faces_in, sides, sides_in, means, means_in, cz, fw, bw, mw,
    local_sem, send_sem, recv_sem,
):
    me = lax.axis_index("gx")
    right, left = lax.rem(me + 1, devices), lax.rem(me + devices - 1, devices)
    cells = state.shape[1]

    loads = [
        pltpu.make_async_copy(state.at[0], fe.at[pl.ds(5, cells)], local_sem.at[0]),
        pltpu.make_async_copy(state.at[1], pe.at[pl.ds(4, cells)], local_sem.at[1]),
        pltpu.make_async_copy(fine, q, local_sem.at[2]),
    ]
    for load in loads:
        load.start()

    barrier = pltpu.get_barrier_semaphore()
    for neighbour in (left, right):
        pl.semaphore_signal(barrier, inc=1, device_id={"gx": neighbour}, device_id_type=MESH)
    pl.semaphore_wait(barrier, 2)

    def remote(src, dst, number, target):
        return pltpu.make_async_remote_copy(
            src_ref=src, dst_ref=dst, send_sem=send_sem.at[number], recv_sem=recv_sem.at[number],
            device_id={"gx": target}, device_id_type=MESH,
        )

    halo = [
        remote(state.at[0, pl.ds(cells - 5, 5)], fe.at[pl.ds(0, 5)], 0, right),
        remote(state.at[0, pl.ds(0, 5)], fe.at[pl.ds(cells + 5, 5)], 1, left),
        remote(state.at[1, pl.ds(cells - 4, 4)], pe.at[pl.ds(0, 4)], 2, right),
        remote(state.at[1, pl.ds(0, 4)], pe.at[pl.ds(cells + 4, 4)], 3, left),
    ]
    for copy in halo:
        copy.start()

    cz[...] = coarse_weights()
    inner, outer = fine_weights()
    fw[0:256] = inner
    fw[256:512] = outer
    wy, wzl, wzh, wx = boundary_weights()
    bw[0] = wy
    bw[1] = wzl
    bw[2] = wzh
    bw[3] = wx
    mw[...] = mean_weights()
    zeros8 = jnp.zeros((8, 1024), F32)
    for i in range(2):
        pad[i, 0:8] = zeros8
        pad[i, 40:48] = zeros8

    corner = []
    for dest in range(2):
        holder = me if dest == 0 else right
        for i in range(2):
            number = plan[holder * BOX_DEV + i]
            x, y, z = boxes[number, 0], boxes[number, 1], boxes[number, 2]
            corner.append((jnp.where(lax.div(x, jnp.int32(cells)) == me, 1, 0), y, z))

    def pick(index, values):
        out = values[-1]
        for number in range(len(values) - 2, -1, -1):
            out = jnp.where(index == number, values[number], out)
        return out

    def force(ref, base, start, n):
        at = start - base
        centre = ref[pl.ds(at, n)]
        near = ref[pl.ds(at - 1, n)] + ref[pl.ds(at + 1, n)]
        far = ref[pl.ds(at - 2, n)] + ref[pl.ds(at + 2, n)]
        near += roll(centre, 1, 1) + roll(centre, -1, 1)
        far += roll(centre, 2, 1) + roll(centre, -2, 1)
        hi, lo = halves(centre.reshape(n * 32, 256))
        along_z = (mm(hi, cz[...]) + mm(lo, cz[...])).reshape(n, 32, 256)
        lap = (16.0 * near - far + along_z - 90.0 * centre) * (1.0 / 12.0)
        return lap + centre * (centre * centre - 1.0)

    def fill_f2(start, n):
        f2[pl.ds(start + 4, n)] = fe[pl.ds(start + 5, n)] + 0.25 * pe[pl.ds(start + 4, n)]

    def stage1(start, n):
        slope = force(fe, -5, start, n)
        k1[pl.ds(start + 3, n)] = slope
        f3[pl.ds(start + 3, n)] = f2[pl.ds(start + 4, n)] + 0.0625 * slope

    def stage2(start, n):
        slope = force(f2, -4, start, n)
        k2[pl.ds(start + 2, n)] = slope
        f4[pl.ds(start + 2, n)] = fe[pl.ds(start + 5, n)] + 0.5 * pe[pl.ds(start + 4, n)] + 0.125 * slope

    def stage3(start, n):
        slope = force(f3, -3, start, n)
        one, two = k1[pl.ds(start + 3, n)], k2[pl.ds(start + 2, n)]
        nf[pl.ds(start + 1, n)] = (
            fe[pl.ds(start + 5, n)] + 0.5 * pe[pl.ds(start + 4, n)] + (1.0 / 24.0) * (one + two + slope)
        )
        k2[pl.ds(start + 2, n)] = one + 2.0 * two + 2.0 * slope

    def stage4(start, n):
        slope = force(f4, -2, start, n)
        npm[pl.ds(start, n)] = pe[pl.ds(start + 4, n)] + (1.0 / 12.0) * (k2[pl.ds(start + 2, n)] + slope)

    loads[0].wait()
    loads[1].wait()
    for s in range(0, 16, 4):
        fill_f2(s, 4)
    for s in range(2, 14, 4):
        stage1(s, 4)
        stage2(s, 4)
    loads[2].wait()
    for copy in halo:
        copy.wait()
    for s in (-4, 16):
        fill_f2(s, 4)
    for s in (-3, 14):
        stage1(s, 5)
    for s in (-2, 14):
        stage2(s, 4)
    for s in range(-1, 17, 6):
        stage3(s, 6)

    lane = iota((1, 128), 1)
    group = ((lane >> 6) << 1) + ((lane >> 4) & 1)
    lane_y = pick(group, [c[1] for c in corner])
    lane_z = pick(group, [c[2] for c in corner]) + (lane & 15)
    k = iota((256, 128), 0)
    hit = jnp.where(k == lane_z, 1.0, 0.0)
    raw = None
    rows8 = iota((8, 1), 0)
    row_box = rows8 >> 1
    row_y = pick(row_box, [c[1] for c in corner])
    row_z = pick(row_box, [c[2] for c in corner])
    row_z = jnp.where((rows8 & 1) == 0, row_z + 255, row_z + 16) & 255
    side_hit = jnp.where(iota((8, 256), 1) == row_z, 1.0, 0.0).astype(BF)
    for t, (ref, base) in enumerate(((fe, 4), (nf, 0))):
        body = ref[pl.ds(base + 1, cells)]
        rows = jnp.concatenate(
            [ref[base], ref[base + cells + 1], body[:, 31], body[:, 15], body[:, 16], body[:, 0]], axis=0
        )
        hi, lo = halves(rows)
        weight = jnp.where(((iota((256, 128), 1) >> 5) & 1) == t, hit, 0.0).astype(BF)
        part = mm(hi, weight) + mm(lo, weight)
        raw = part if raw is None else raw + part
        hi, lo = halves(body.reshape(cells * 32, 256))
        side = mm_nt(side_hit, hi) + mm_nt(side_hit, lo)
        sides[pl.ds(8 * t, 8)] = jnp.where(jnp.broadcast_to(row_y, (8, 512)) == 0, side, roll(side, -16, 1))
    low = jnp.broadcast_to(lane_y, (16, 128)) == 0
    faces[0:16] = jnp.where(low, raw[0:16], raw[16:32])
    faces[16:32] = jnp.where(low, raw[32:48], raw[48:64])
    faces[32:48] = jnp.where(low, raw[64:80], raw[80:96])
    faces[48:64] = jnp.where(low, raw[96:112], raw[112:128])
    patch = [remote(faces, faces_in, 4, right), remote(sides, sides_in, 5, right)]
    for copy in patch:
        copy.start()

    for s in range(0, 16, 4):
        stage4(s, 4)

    def inside(f):
        for i in range(2):
            pad[i, 8:40] = f[32 * i : 32 * i + 32]
        hi, lo = halves(f)
        none = jnp.zeros((64, 128), BF)

        def gathered(a):
            mid = jnp.concatenate([a[:, 256 * t : 256 * t + 256] for t in range(4)], axis=0)
            before = [none] + [a[:, 256 * t - 128 : 256 * t] for t in range(1, 4)]
            after = [a[:, 256 * t + 256 : 256 * t + 384] for t in range(3)] + [none]
            beside = jnp.concatenate(
                [jnp.concatenate(before, axis=0), jnp.concatenate(after, axis=0)], axis=1
            )
            return jnp.concatenate([mid, beside], axis=1)

        weights = fw[...]
        out = mm(gathered(hi), weights) + mm(gathered(lo), weights)
        along = jnp.concatenate([out[64 * t : 64 * t + 64] for t in range(4)], axis=1)

        def shifted(d):
            return jnp.concatenate([pad[i, 8 + d : 40 + d] for i in range(2)], axis=0)

        lap = 16.0 * (shifted(1) + shifted(-1)) - (shifted(2) + shifted(-2)) + along - 90.0 * f
        return lap * (1.0 / 3.0) + f * (f * f - 1.0)

    h = 0.25
    f = q[0].reshape(64, 1024)
    p = q[1].reshape(64, 1024)
    first = inside(f)
    second = inside(f + (h / 2) * p)

    for copy in patch:
        copy.wait()
    own = [c[0] for c in corner[:2]]
    lane_own = pick((lane >> 4) & 1, own)
    mixed = jnp.where(jnp.broadcast_to(lane_own, (64, 128)) == 1, faces[...], roll(faces_in[...], 64, 1))
    wide_lane = iota((128, 128), 1)
    same_group = ((wide_lane >> 4) & 3) == (iota((128, 128), 0) >> 5)
    y_faces = jnp.where(iota((16, 128), 1) < 64, mixed[32:48], roll(mixed[48:64], 64, 1))
    up = jnp.where(((iota((128, 16), 0) & 31) >> 1) == iota((128, 16), 1), 1.0, 0.0).astype(BF)
    hi, lo = halves(y_faces)
    wide = mm(up, hi) + mm(up, lo)
    wide = jnp.where(same_group, wide, 0.0)
    hi, lo = halves(wide)
    bound = mm(hi, bw[0]) + mm(lo, bw[0])
    stripe = (iota((8, 128), 1) >> 5) == (iota((8, 128), 0) >> 1)
    for side in range(2):
        blocks = []
        for t in range(2):
            for i in range(2):
                at = 8 * t + 2 * i + side
                line = jnp.where(own[i] == 1, sides[pl.ds(at, 1)], sides_in[pl.ds(at + 4, 1)])
                for tile in range(4):
                    piece = line[:, 128 * tile : 128 * tile + 128]
                    blocks.append(jnp.where(stripe, jnp.broadcast_to(piece, (8, 128)), 0.0))
        hi, lo = halves(jnp.concatenate(blocks, axis=0))
        bound += mm(hi, bw[1 + side]) + mm(lo, bw[1 + side])
    x_faces = jnp.concatenate([mixed[0:32]] * 4, axis=0)
    x_faces = jnp.where(same_group & (wide_lane < 64), x_faces, 0.0)
    hi, lo = halves(x_faces)
    spread = mm(hi, bw[3]) + mm(lo, bw[3])
    fits = (iota((128, 1024), 0) & 15) == (iota((128, 1024), 1) >> 6)
    spread = jnp.where(fits, spread, 0.0)
    kk, rr = iota((128, 128), 1), iota((128, 128), 0)
    lift = jnp.where((kk >> 5) == (rr >> 5), edge((kk >> 4) & 1, rr & 31), 0.0).astype(BF)
    hi, lo = halves(spread)
    bound += mm(lift, hi) + mm(lift, lo)
    bound = bound * (1.0 / 3.0)
    b_old = bound[0:64]
    b_diff = bound[64:128] - b_old

    for step in range(2):
        r = 0.5 * step
        if step == 1:
            first = inside(f)
            second = inside(f + (h / 2) * p)
        one = first + (b_old + r * b_diff)
        mid = b_old + (r + 0.25) * b_diff
        two = second + mid
        three = inside(f + (h / 2) * p + (h * h / 4) * one) + mid
        four = inside(f + h * p + (h * h / 2) * two) + (b_old + (r + 0.5) * b_diff)
        f = f + h * p + (h * h / 6) * (one + two + three)
        p = p + (h / 6) * (one + 2.0 * two + 2.0 * three + four)
    q[0] = f.reshape(2, 32, 1024)
    q[1] = p.reshape(2, 32, 1024)
    store_fine = pltpu.make_async_copy(q, fine_out, local_sem.at[2])
    store_fine.start()

    hi, lo = halves(jnp.concatenate([f, p], axis=0))
    flat = mm(hi, mw[...]) + mm(lo, mw[...])
    pair = jnp.where((iota((64, 128), 1) >> 1) == iota((64, 128), 0), 0.125, 0.0).astype(BF)
    hi, lo = halves(flat)
    means[...] = mm(pair, hi) + mm(pair, lo)
    back = remote(means, means_in, 6, left)
    back.start()

    eye = (iota((8, 128), 1) >> 4) == iota((8, 128), 0)
    z_lane = iota((16, 16, 256), 2)

    def insert(ref, i, keep, y, z):
        blocks = []
        for c in range(2):
            values = ref[pl.ds(32 * c + 16 * i, 16)]
            for x in range(16):
                for tile in range(2):
                    piece = values[x : x + 1, 128 * tile : 128 * tile + 128]
                    blocks.append(jnp.where(eye, jnp.broadcast_to(piece, (8, 128)), 0.0))
        hi, lo = halves(jnp.concatenate(blocks, axis=0))
        place = jnp.where((iota((128, 256), 0) & 15) + z == iota((128, 256), 1), 1.0, 0.0).astype(BF)
        block = (mm(hi, place) + mm(lo, place)).reshape(2, 16, 16, 256)
        for half in range(2):
            chosen = jnp.where(y == 16 * half, keep, 0)
            here = jnp.where((z_lane >> 4) == (z >> 4), chosen, 0) == 1
            rows = pl.ds(16 * half, 16)
            nf[pl.ds(1, cells), rows] = jnp.where(here, block[0], nf[pl.ds(1, cells), rows])
            npm[:, rows] = jnp.where(here, block[1], npm[:, rows])

    for i in range(2):
        insert(means, i, *corner[i])
    back.wait()
    for i in range(2):
        insert(means_in, i, *corner[2 + i])
    stores = [
        pltpu.make_async_copy(nf.at[pl.ds(1, cells)], coarse_out.at[0], local_sem.at[0]),
        pltpu.make_async_copy(npm, coarse_out.at[1], local_sem.at[1]),
    ]
    for store in stores:
        store.start()
    store_fine.wait()
    for store in stores:
        store.wait()


def shards(devices, state, fine_state, box_list, plan):
    cells, ny, nz = state.shape[1:]

    def slab(layers):
        return pltpu.VMEM((layers, ny, nz), F32)

    any_spec = pl.BlockSpec(memory_space=pl.ANY)
    smem_spec = pl.BlockSpec(memory_space=pltpu.SMEM)

    def body(*refs):
        kernel(devices, *refs)

    return pl.pallas_call(
        body,
        out_shape=(
            jax.ShapeDtypeStruct(state.shape, F32),
            jax.ShapeDtypeStruct(fine_state.shape, F32),
        ),
        in_specs=[any_spec, any_spec, smem_spec, smem_spec],
        out_specs=(any_spec, any_spec),
        scratch_shapes=[
            slab(cells + 10), slab(cells + 8),
            slab(cells + 8), slab(cells + 6), slab(cells + 4),
            slab(cells + 6), slab(cells + 4), slab(cells + 2), slab(cells),
            pltpu.VMEM(fine_state.shape, F32),
            pltpu.VMEM((2, 48, 1024), F32),
            pltpu.VMEM((64, 128), F32), pltpu.VMEM((64, 128), F32),
            pltpu.VMEM((16, 512), F32), pltpu.VMEM((16, 512), F32),
            pltpu.VMEM((64, 256), F32), pltpu.VMEM((64, 256), F32),
            pltpu.VMEM((256, 256), BF), pltpu.VMEM((512, 256), BF),
            pltpu.VMEM((4, 128, 1024), BF), pltpu.VMEM((1024, 256), BF),
            pltpu.SemaphoreType.DMA((3,)),
            pltpu.SemaphoreType.DMA((7,)),
            pltpu.SemaphoreType.DMA((7,)),
        ],
        compiler_params=pltpu.CompilerParams(
            collective_id=0, has_side_effects=True, vmem_limit_bytes=48 * 1024 * 1024
        ),
        cost_estimate=pl.CostEstimate(flops=10**9, bytes_accessed=3 * 2**20, transcendentals=0),
        name="refined_step",
    )(state, fine_state, box_list, plan)


def solution(mesh):
    devices = mesh.shape["gx"]

    def local(*args):
        return shards(devices, *args)

    return jax.shard_map(
        local,
        mesh=mesh,
        in_specs=(
            P(None, ("ens", "gx"), None, None),
            P(None, ("ens", "gx"), None, None),
            P("ens", None),
            P("ens"),
        ),
        out_specs=(P(None, ("ens", "gx"), None, None), P(None, ("ens", "gx"), None, None)),
        check_vma=False,
    )
```

profile of v0, /device:TPU:0, one launch (start us, length us, event | category | flops | bytes accessed | tf_op | source)
XLA Modules:
  0.0 31.5 jit_solution(7169696624416623889)
XLA Ops:
  0.6 0.0 copy-start.2
  0.6 0.8 %copy.6.refs_2_ = s32[32,3]{1,0:T(8,128)S(1)} copy(s32[32,3]{0,1:T(4,128)} %param.6) | data formatting | bytes 768 | tf_op args[2]
  1.4 0.0 copy-done.2
  1.4 0.0 copy-start
  1.4 1.2 %copy-done = f32[2,16,32,256]{3,2,1,0:T(8,128)S(1)} copy-done((f32[2,16,32,256]{3,2,1,0:T(8,128)S(1)}, f32[2,16,32,256]{3,2,1,0:T(8,128)}, u32[]{:S(2)}) %copy-start) | copy-done | bytes 1048600
  2.6 0.0 copy-start.1
  2.6 1.0 %copy-done.1 = f32[2,2,32,1024]{3,2,1,0:T(8,128)S(1)} copy-done((f32[2,2,32,1024]{3,2,1,0:T(8,128)S(1)}, f32[2,2,32,1024]{3,2,1,0:T(8,128)}, u32[]{:S(2)}) %copy-start.1) | copy-done | bytes 524312
  3.7 26.1 %refined_step.1 = (f32[2,16,32,256]{3,2,1,0:T(8,128)S(1)}, f32[2,2,32,1024]{3,2,1,0:T(8,128)S(1)}) custom-call(f32[2,16,32,256]{3,2,1,0:T(8,128)S(1)} %copy-done, f32[2,2,32,1024]{3,2,1,0:T(8,128)S(1)} %copy-done.1, s32[32,3]{1,0:T(8,128)S(1)} %copy.6.refs_2_, s32[32]{0:T(128)S(1)} %copy-done.2), custom_call_target="tpu_custom_call" | custom-call | flops 1000000000 | bytes 3145728 | tf_op jit(solution)/shard_map/refined_step/pallas_call | solution.py:386
  29.8 1.0 %copy.9 = f32[2,16,32,256]{3,2,1,0:T(8,128)} copy(f32[2,16,32,256]{3,2,1,0:T(8,128)S(1)} %get-tuple-element.4) | data formatting | bytes 2097152
  30.7 0.8 %copy.10 = f32[2,2,32,1024]{3,2,1,0:T(8,128)} copy(f32[2,2,32,1024]{3,2,1,0:T(8,128)S(1)} %get-tuple-element.5) | data formatting | bytes 1048576
Async XLA Ops:
  0.6 0.8 %copy-start.2 = (s32[32]{0:T(128)S(1)}, s32[32]{0:T(128)}, u32[]{:S(2)}) copy-start(s32[32]{0:T(128)} %refs_3_.1) | copy-start | bytes 388
  1.4 1.2 %copy-start = (f32[2,16,32,256]{3,2,1,0:T(8,128)S(1)}, f32[2,16,32,256]{3,2,1,0:T(8,128)}, u32[]{:S(2)}) copy-start(f32[2,16,32,256]{3,2,1,0:T(8,128)} %refs_0_.1) | copy-start | bytes 3145732
  2.6 1.0 %copy-start.1 = (f32[2,2,32,1024]{3,2,1,0:T(8,128)S(1)}, f32[2,2,32,1024]{3,2,1,0:T(8,128)}, u32[]{:S(2)}) copy-start(f32[2,2,32,1024]{3,2,1,0:T(8,128)} %refs_1_.1) | copy-start | bytes 1572868
where the time goes:
time: 31.8 us; the launch traced here: 31.5 us
  Pallas kernels  26.1 us (82%)
  local copies, waits for them, and re-layouts  4.8 us (15%)
  between operations  0.65 us (2%)
    pallas_call x1, Pallas kernels, shards(): pl.pallas_call(body, out_shape=(jax.ShapeDtypeStruct(state.shape, F32), j...  26.1 us
    unnamed x9, local copies, waits for them, and re-layouts  4.8 us

commit v1 on v0

--- a/solution.py
+++ b/solution.py
@@ -78,27 +78,29 @@
 
 def kernel(
     devices,
-    state, fine, boxes, plan,
+    state, fine, boxes_hbm, plan_hbm,
     coarse_out, fine_out,
     fe, pe, f2, f3, f4, k1, k2, nf, npm,
-    q, pad, faces, faces_in, sides, sides_in, means, means_in, cz, fw, bw, mw,
+    q, pad, patches, patches_in, means, means_in, cz, fw, bw, mw, boxes, plan,
     local_sem, send_sem, recv_sem,
 ):
     me = lax.axis_index("gx")
     right, left = lax.rem(me + 1, devices), lax.rem(me + devices - 1, devices)
     cells = state.shape[1]
 
+    barrier = pltpu.get_barrier_semaphore()
+    for neighbour in (left, right):
+        pl.semaphore_signal(barrier, inc=1, device_id={"gx": neighbour}, device_id_type=MESH)
     loads = [
         pltpu.make_async_copy(state.at[0], fe.at[pl.ds(5, cells)], local_sem.at[0]),
         pltpu.make_async_copy(state.at[1], pe.at[pl.ds(4, cells)], local_sem.at[1]),
         pltpu.make_async_copy(fine, q, local_sem.at[2]),
+        pltpu.make_async_copy(boxes_hbm, boxes, local_sem.at[3]),
+        pltpu.make_async_copy(plan_hbm, plan, local_sem.at[4]),
     ]
     for load in loads:
         load.start()
 
-    barrier = pltpu.get_barrier_semaphore()
-    for neighbour in (left, right):
-        pl.semaphore_signal(barrier, inc=1, device_id={"gx": neighbour}, device_id_type=MESH)
     pl.semaphore_wait(barrier, 2)
 
     def remote(src, dst, number, target):
@@ -131,12 +133,14 @@
         pad[i, 0:8] = zeros8
         pad[i, 40:48] = zeros8
 
+    loads[3].wait()
+    loads[4].wait()
     corner = []
     for dest in range(2):
         holder = me if dest == 0 else right
         for i in range(2):
             number = plan[holder * BOX_DEV + i]
-            x, y, z = boxes[number, 0], boxes[number, 1], boxes[number, 2]
+            x, y, z = boxes[0, number], boxes[1, number], boxes[2, number]
             corner.append((jnp.where(lax.div(x, jnp.int32(cells)) == me, 1, 0), y, z))
 
     def pick(index, values):
@@ -189,7 +193,41 @@
     for s in range(2, 14, 4):
         stage1(s, 4)
         stage2(s, 4)
+    stage3(4, 4)
+    stage3(8, 4)
     loads[2].wait()
+
+    def inside(f):
+        for i in range(2):
+            pad[i, 8:40] = f[32 * i : 32 * i + 32]
+        hi, lo = halves(f)
+        none = jnp.zeros((64, 128), BF)
+
+        def gathered(a):
+            mid = jnp.concatenate([a[:, 256 * t : 256 * t + 256] for t in range(4)], axis=0)
+            before = [none] + [a[:, 256 * t - 128 : 256 * t] for t in range(1, 4)]
+            after = [a[:, 256 * t + 256 : 256 * t + 384] for t in range(3)] + [none]
+            beside = jnp.concatenate(
+                [jnp.concatenate(before, axis=0), jnp.concatenate(after, axis=0)], axis=1
+            )
+            return jnp.concatenate([mid, beside], axis=1)
+
+        weights = fw[...]
+        out = mm(gathered(hi), weights) + mm(gathered(lo), weights)
+        along = jnp.concatenate([out[64 * t : 64 * t + 64] for t in range(4)], axis=1)
+
+        def shifted(d):
+            return jnp.concatenate([pad[i, 8 + d : 40 + d] for i in range(2)], axis=0)
+
+        lap = 16.0 * (shifted(1) + shifted(-1)) - (shifted(2) + shifted(-2)) + along - 90.0 * f
+        return lap * (1.0 / 3.0) + f * (f * f - 1.0)
+
+    h = 0.25
+    f = q[0].reshape(64, 1024)
+    p = q[1].reshape(64, 1024)
+    first = inside(f)
+    second = inside(f + (h / 2) * p)
+
     for copy in halo:
         copy.wait()
     for s in (-4, 16):
@@ -198,8 +236,8 @@
         stage1(s, 5)
     for s in (-2, 14):
         stage2(s, 4)
-    for s in range(-1, 17, 6):
-        stage3(s, 6)
+    for s in (-1, 12):
+        stage3(s, 5)
 
     lane = iota((1, 128), 1)
     group = ((lane >> 6) << 1) + ((lane >> 4) & 1)
@@ -225,58 +263,37 @@
         raw = part if raw is None else raw + part
         hi, lo = halves(body.reshape(cells * 32, 256))
         side = mm_nt(side_hit, hi) + mm_nt(side_hit, lo)
-        sides[pl.ds(8 * t, 8)] = jnp.where(jnp.broadcast_to(row_y, (8, 512)) == 0, side, roll(side, -16, 1))
+        side = jnp.where(jnp.broadcast_to(row_y, (8, 512)) == 0, side, roll(side, -16, 1))
+        for dest in range(2):
+            for tile in range(4):
+                patches[dest, pl.ds(32 + 8 * tile + 4 * t, 4)] = side[
+                    4 * dest : 4 * dest + 4, 128 * tile : 128 * tile + 128
+                ]
     low = jnp.broadcast_to(lane_y, (16, 128)) == 0
-    faces[0:16] = jnp.where(low, raw[0:16], raw[16:32])
-    faces[16:32] = jnp.where(low, raw[32:48], raw[48:64])
-    faces[32:48] = jnp.where(low, raw[64:80], raw[80:96])
-    faces[48:64] = jnp.where(low, raw[96:112], raw[112:128])
-    patch = [remote(faces, faces_in, 4, right), remote(sides, sides_in, 5, right)]
+    x_part = jnp.concatenate(
+        [jnp.where(low, raw[0:16], raw[16:32]), jnp.where(low, raw[32:48], raw[48:64])], axis=0
+    )
+    y_part = jnp.concatenate(
+        [jnp.where(low, raw[64:80], raw[80:96]), jnp.where(low, raw[96:112], raw[112:128])], axis=0
+    )
+    first_half = iota((32, 128), 1) < 64
+    patches[0, 0:32] = jnp.where(first_half, x_part, roll(y_part, 64, 1))
+    patches[1, 0:32] = jnp.where(first_half, roll(x_part, 64, 1), y_part)
+    patch = [remote(patches.at[1], patches_in, 4, right)]
     for copy in patch:
         copy.start()
 
     for s in range(0, 16, 4):
         stage4(s, 4)
-
-    def inside(f):
-        for i in range(2):
-            pad[i, 8:40] = f[32 * i : 32 * i + 32]
-        hi, lo = halves(f)
-        none = jnp.zeros((64, 128), BF)
-
-        def gathered(a):
-            mid = jnp.concatenate([a[:, 256 * t : 256 * t + 256] for t in range(4)], axis=0)
-            before = [none] + [a[:, 256 * t - 128 : 256 * t] for t in range(1, 4)]
-            after = [a[:, 256 * t + 256 : 256 * t + 384] for t in range(3)] + [none]
-            beside = jnp.concatenate(
-                [jnp.concatenate(before, axis=0), jnp.concatenate(after, axis=0)], axis=1
-            )
-            return jnp.concatenate([mid, beside], axis=1)
-
-        weights = fw[...]
-        out = mm(gathered(hi), weights) + mm(gathered(lo), weights)
-        along = jnp.concatenate([out[64 * t : 64 * t + 64] for t in range(4)], axis=1)
-
-        def shifted(d):
-            return jnp.concatenate([pad[i, 8 + d : 40 + d] for i in range(2)], axis=0)
-
-        lap = 16.0 * (shifted(1) + shifted(-1)) - (shifted(2) + shifted(-2)) + along - 90.0 * f
-        return lap * (1.0 / 3.0) + f * (f * f - 1.0)
-
-    h = 0.25
-    f = q[0].reshape(64, 1024)
-    p = q[1].reshape(64, 1024)
-    first = inside(f)
-    second = inside(f + (h / 2) * p)
 
     for copy in patch:
         copy.wait()
     own = [c[0] for c in corner[:2]]
     lane_own = pick((lane >> 4) & 1, own)
-    mixed = jnp.where(jnp.broadcast_to(lane_own, (64, 128)) == 1, faces[...], roll(faces_in[...], 64, 1))
+    mixed = jnp.where(jnp.broadcast_to(lane_own, (32, 128)) == 1, patches[0, 0:32], patches_in[0:32])
     wide_lane = iota((128, 128), 1)
     same_group = ((wide_lane >> 4) & 3) == (iota((128, 128), 0) >> 5)
-    y_faces = jnp.where(iota((16, 128), 1) < 64, mixed[32:48], roll(mixed[48:64], 64, 1))
+    y_faces = jnp.where(iota((16, 128), 1) < 64, roll(mixed[0:16], 64, 1), mixed[16:32])
     up = jnp.where(((iota((128, 16), 0) & 31) >> 1) == iota((128, 16), 1), 1.0, 0.0).astype(BF)
     hi, lo = halves(y_faces)
     wide = mm(up, hi) + mm(up, lo)
@@ -288,14 +305,13 @@
         blocks = []
         for t in range(2):
             for i in range(2):
-                at = 8 * t + 2 * i + side
-                line = jnp.where(own[i] == 1, sides[pl.ds(at, 1)], sides_in[pl.ds(at + 4, 1)])
                 for tile in range(4):
-                    piece = line[:, 128 * tile : 128 * tile + 128]
+                    at = pl.ds(32 + 8 * tile + 4 * t + 2 * i + side, 1)
+                    piece = jnp.where(own[i] == 1, patches[0, at], patches_in[at])
                     blocks.append(jnp.where(stripe, jnp.broadcast_to(piece, (8, 128)), 0.0))
         hi, lo = halves(jnp.concatenate(blocks, axis=0))
         bound += mm(hi, bw[1 + side]) + mm(lo, bw[1 + side])
-    x_faces = jnp.concatenate([mixed[0:32]] * 4, axis=0)
+    x_faces = jnp.concatenate([mixed] * 4, axis=0)
     x_faces = jnp.where(same_group & (wide_lane < 64), x_faces, 0.0)
     hi, lo = halves(x_faces)
     spread = mm(hi, bw[3]) + mm(lo, bw[3])
@@ -309,6 +325,21 @@
     b_old = bound[0:64]
     b_diff = bound[64:128] - b_old
 
+    pair = jnp.where((iota((32, 64), 1) >> 1) == iota((32, 64), 0), 0.125, 0.0).astype(BF)
+    sent = []
+
+    def finish(c, values):
+        q[c] = values.reshape(2, 32, 1024)
+        hi, lo = halves(values)
+        flat = mm(hi, mw[...]) + mm(lo, mw[...])
+        hi, lo = halves(flat)
+        means[c] = mm(pair, hi) + mm(pair, lo)
+        back = remote(means.at[c], means_in.at[c], 5 + c, left)
+        back.start()
+        store = pltpu.make_async_copy(q.at[c], fine_out.at[c], local_sem.at[2 + c])
+        store.start()
+        sent.append((back, store))
+
     for step in range(2):
         r = 0.5 * step
         if step == 1:
@@ -318,67 +349,60 @@
         mid = b_old + (r + 0.25) * b_diff
         two = second + mid
         three = inside(f + (h / 2) * p + (h * h / 4) * one) + mid
+        new = f + h * p + (h * h / 6) * (one + two + three)
+        if step == 1:
+            finish(0, new)
         four = inside(f + h * p + (h * h / 2) * two) + (b_old + (r + 0.5) * b_diff)
-        f = f + h * p + (h * h / 6) * (one + two + three)
+        f = new
         p = p + (h / 6) * (one + 2.0 * two + 2.0 * three + four)
-    q[0] = f.reshape(2, 32, 1024)
-    q[1] = p.reshape(2, 32, 1024)
-    store_fine = pltpu.make_async_copy(q, fine_out, local_sem.at[2])
-    store_fine.start()
-
-    hi, lo = halves(jnp.concatenate([f, p], axis=0))
-    flat = mm(hi, mw[...]) + mm(lo, mw[...])
-    pair = jnp.where((iota((64, 128), 1) >> 1) == iota((64, 128), 0), 0.125, 0.0).astype(BF)
-    hi, lo = halves(flat)
-    means[...] = mm(pair, hi) + mm(pair, lo)
-    back = remote(means, means_in, 6, left)
-    back.start()
+    finish(1, p)
 
     eye = (iota((8, 128), 1) >> 4) == iota((8, 128), 0)
     z_lane = iota((16, 16, 256), 2)
 
-    def insert(ref, i, keep, y, z):
+    into = (nf.at[pl.ds(1, cells)], npm)
+
+    def insert(ref, c, i, keep, y, z):
+        values = ref[c, pl.ds(16 * i, 16)]
         blocks = []
-        for c in range(2):
-            values = ref[pl.ds(32 * c + 16 * i, 16)]
-            for x in range(16):
-                for tile in range(2):
-                    piece = values[x : x + 1, 128 * tile : 128 * tile + 128]
-                    blocks.append(jnp.where(eye, jnp.broadcast_to(piece, (8, 128)), 0.0))
+        for x in range(16):
+            for tile in range(2):
+                piece = values[x : x + 1, 128 * tile : 128 * tile + 128]
+                blocks.append(jnp.where(eye, jnp.broadcast_to(piece, (8, 128)), 0.0))
         hi, lo = halves(jnp.concatenate(blocks, axis=0))
         place = jnp.where((iota((128, 256), 0) & 15) + z == iota((128, 256), 1), 1.0, 0.0).astype(BF)
-        block = (mm(hi, place) + mm(lo, place)).reshape(2, 16, 16, 256)
+        block = (mm(hi, place) + mm(lo, place)).reshape(16, 16, 256)
         for half in range(2):
             chosen = jnp.where(y == 16 * half, keep, 0)
             here = jnp.where((z_lane >> 4) == (z >> 4), chosen, 0) == 1
             rows = pl.ds(16 * half, 16)
-            nf[pl.ds(1, cells), rows] = jnp.where(here, block[0], nf[pl.ds(1, cells), rows])
-            npm[:, rows] = jnp.where(here, block[1], npm[:, rows])
-
-    for i in range(2):
-        insert(means, i, *corner[i])
-    back.wait()
-    for i in range(2):
-        insert(means_in, i, *corner[2 + i])
-    stores = [
-        pltpu.make_async_copy(nf.at[pl.ds(1, cells)], coarse_out.at[0], local_sem.at[0]),
-        pltpu.make_async_copy(npm, coarse_out.at[1], local_sem.at[1]),
-    ]
-    for store in stores:
+            into[c][:, rows] = jnp.where(here, block, into[c][:, rows])
+
+    stores = []
+    for c in range(2):
+        for i in range(2):
+            insert(means, c, i, *corner[i])
+    for c in range(2):
+        sent[c][0].wait()
+        for i in range(2):
+            insert(means_in, c, i, *corner[2 + i])
+        store = pltpu.make_async_copy(into[c], coarse_out.at[c], local_sem.at[c])
         store.start()
-    store_fine.wait()
-    for store in stores:
-        store.wait()
+        stores.append(store)
+    for c in range(2):
+        sent[c][1].wait()
+        stores[c].wait()
 
 
 def shards(devices, state, fine_state, box_list, plan):
+    boxes = box_list.T
     cells, ny, nz = state.shape[1:]
 
     def slab(layers):
         return pltpu.VMEM((layers, ny, nz), F32)
 
     any_spec = pl.BlockSpec(memory_space=pl.ANY)
-    smem_spec = pl.BlockSpec(memory_space=pltpu.SMEM)
+    hbm_spec = pl.BlockSpec(memory_space=pltpu.HBM)
 
     def body(*refs):
         kernel(devices, *refs)
@@ -389,7 +413,7 @@
             jax.ShapeDtypeStruct(state.shape, F32),
             jax.ShapeDtypeStruct(fine_state.shape, F32),
         ),
-        in_specs=[any_spec, any_spec, smem_spec, smem_spec],
+        in_specs=[hbm_spec, hbm_spec, hbm_spec, hbm_spec],
         out_specs=(any_spec, any_spec),
         scratch_shapes=[
             slab(cells + 10), slab(cells + 8),
@@ -397,12 +421,12 @@
             slab(cells + 6), slab(cells + 4), slab(cells + 2), slab(cells),
             pltpu.VMEM(fine_state.shape, F32),
             pltpu.VMEM((2, 48, 1024), F32),
-            pltpu.VMEM((64, 128), F32), pltpu.VMEM((64, 128), F32),
-            pltpu.VMEM((16, 512), F32), pltpu.VMEM((16, 512), F32),
-            pltpu.VMEM((64, 256), F32), pltpu.VMEM((64, 256), F32),
+            pltpu.VMEM((2, 64, 128), F32), pltpu.VMEM((64, 128), F32),
+            pltpu.VMEM((2, 32, 256), F32), pltpu.VMEM((2, 32, 256), F32),
             pltpu.VMEM((256, 256), BF), pltpu.VMEM((512, 256), BF),
             pltpu.VMEM((4, 128, 1024), BF), pltpu.VMEM((1024, 256), BF),
-            pltpu.SemaphoreType.DMA((3,)),
+            pltpu.SMEM(boxes.shape, jnp.int32), pltpu.SMEM(plan.shape, jnp.int32),
+            pltpu.SemaphoreType.DMA((5,)),
             pltpu.SemaphoreType.DMA((7,)),
             pltpu.SemaphoreType.DMA((7,)),
         ],
@@ -411,7 +435,7 @@
         ),
         cost_estimate=pl.CostEstimate(flops=10**9, bytes_accessed=3 * 2**20, transcendentals=0),
         name="refined_step",
-    )(state, fine_state, box_list, plan)
+    )(state, fine_state, boxes, plan)
 
 
 def solution(mesh):

time: 31.8 us -> 30.6 us (0.962)
  Pallas kernels: 26.1 us -> 24.4 us
  local copies, waits for them, and re-layouts: 4.8 us -> 5.36 us
    pallas_call x1, Pallas kernels: 26.1 us -> 24.4 us  [shards(): pl.pallas_call(body, out_shape=(jax.ShapeDtypeStruct(state.shape, F32), j...]
    unnamed x9 -> x10, local copies, waits for them, and re-layouts: 4.8 us -> 5.36 us
where the time goes in v1:
time: 30.6 us; the launch traced here: 30.4 us
  Pallas kernels  24.4 us (80%)
  local copies, waits for them, and re-layouts  5.36 us (18%)
  between operations  0.65 us (2%)
    pallas_call x1, Pallas kernels, shards(): pl.pallas_call(body, out_shape=(jax.ShapeDtypeStruct(state.shape, F32), j...  24.4 us
    unnamed x10, local copies, waits for them, and re-layouts  5.36 us

profile of v1, /device:TPU:0, one launch (start us, length us, event | category | flops | bytes accessed | tf_op | source)
XLA Modules:
  0.0 30.4 jit_solution(10505675083400641023)
XLA Ops:
  0.6 0.0 copy-start.3
  0.6 0.6 %copy-done.3 = s32[32]{0:T(128)S(1)} copy-done((s32[32]{0:T(128)S(1)}, s32[32]{0:T(128)}, u32[]{:S(2)}) %copy-start.3) | copy-done | bytes 152
  1.3 0.0 copy-start
  1.3 1.2 %copy-done = f32[2,16,32,256]{3,2,1,0:T(8,128)S(1)} copy-done((f32[2,16,32,256]{3,2,1,0:T(8,128)S(1)}, f32[2,16,32,256]{3,2,1,0:T(8,128)}, u32[]{:S(2)}) %copy-start) | copy-done | bytes 1048600
  2.5 0.0 copy-start.1
  2.5 1.0 %copy-done.1 = f32[2,2,32,1024]{3,2,1,0:T(8,128)S(1)} copy-done((f32[2,2,32,1024]{3,2,1,0:T(8,128)S(1)}, f32[2,2,32,1024]{3,2,1,0:T(8,128)}, u32[]{:S(2)}) %copy-start.1) | copy-done | bytes 524312
  3.6 0.0 copy-start.2
  3.6 0.7 %copy-done.2 = s32[32,3]{0,1:T(4,128)S(1)} copy-done((s32[32,3]{0,1:T(4,128)S(1)}, s32[32,3]{0,1:T(4,128)}, u32[]{:S(2)}) %copy-start.2) | copy-done | bytes 408
  4.2 24.4 %refined_step.1 = (f32[2,16,32,256]{3,2,1,0:T(8,128)S(1)}, f32[2,2,32,1024]{3,2,1,0:T(8,128)S(1)}) custom-call(f32[2,16,32,256]{3,2,1,0:T(8,128)S(1)} %copy-done, f32[2,2,32,1024]{3,2,1,0:T(8,128)S(1)} %copy-done.1, s32[3,32]{1,0:T(4,128)S(1)} %bitcast.1, s32[32]{0:T(128)S(1)} %copy-done.3), custom_call_target="tpu_custom_call" | custom-call | flops 1000000000 | bytes 3145728 | tf_op jit(solution)/shard_map/refined_step/pallas_call | solution.py:410
  28.6 1.0 %copy.8 = f32[2,16,32,256]{3,2,1,0:T(8,128)} copy(f32[2,16,32,256]{3,2,1,0:T(8,128)S(1)} %get-tuple-element.4) | data formatting | bytes 2097152
  29.6 0.8 %copy.9 = f32[2,2,32,1024]{3,2,1,0:T(8,128)} copy(f32[2,2,32,1024]{3,2,1,0:T(8,128)S(1)} %get-tuple-element.5) | data formatting | bytes 1048576
Async XLA Ops:
  0.6 0.7 %copy-start.3 = (s32[32]{0:T(128)S(1)}, s32[32]{0:T(128)}, u32[]{:S(2)}) copy-start(s32[32]{0:T(128)} %refs_3_.1) | copy-start | bytes 388
  1.3 1.2 %copy-start = (f32[2,16,32,256]{3,2,1,0:T(8,128)S(1)}, f32[2,16,32,256]{3,2,1,0:T(8,128)}, u32[]{:S(2)}) copy-start(f32[2,16,32,256]{3,2,1,0:T(8,128)} %refs_0_.1) | copy-start | bytes 3145732
  2.5 1.0 %copy-start.1 = (f32[2,2,32,1024]{3,2,1,0:T(8,128)S(1)}, f32[2,2,32,1024]{3,2,1,0:T(8,128)}, u32[]{:S(2)}) copy-start(f32[2,2,32,1024]{3,2,1,0:T(8,128)} %refs_1_.1) | copy-start | bytes 1572868
  3.6 0.7 %copy-start.2 = (s32[32,3]{0,1:T(4,128)S(1)}, s32[32,3]{0,1:T(4,128)}, u32[]{:S(2)}) copy-start(s32[32,3]{0,1:T(4,128)} %param.6) | copy-start | bytes 1156

commit v2 on v1

--- a/solution.py
+++ b/solution.py
@@ -7,6 +7,7 @@
 
 FB = 32
 BOX_DEV = 2
+VMEM_LIMIT = 62 * 1024 * 1024
 MESH = pl.DeviceIdType.MESH
 BF = jnp.bfloat16
 F32 = jnp.float32
@@ -80,7 +81,7 @@
     devices,
     state, fine, boxes_hbm, plan_hbm,
     coarse_out, fine_out,
-    fe, pe, f2, f3, f4, k1, k2, nf, npm,
+    fe, pe, f2, f3, f4, k1, k2, nf,
     q, pad, patches, patches_in, means, means_in, cz, fw, bw, mw, boxes, plan,
     local_sem, send_sem, recv_sem,
 ):
@@ -184,7 +185,7 @@
 
     def stage4(start, n):
         slope = force(f4, -2, start, n)
-        npm[pl.ds(start, n)] = pe[pl.ds(start + 4, n)] + (1.0 / 12.0) * (k2[pl.ds(start + 2, n)] + slope)
+        coarse_out[1, pl.ds(start, n)] = pe[pl.ds(start + 4, n)] + (1.0 / 12.0) * (k2[pl.ds(start + 2, n)] + slope)
 
     loads[0].wait()
     loads[1].wait()
@@ -283,6 +284,8 @@
     for copy in patch:
         copy.start()
 
+    new_field = pltpu.make_async_copy(nf.at[pl.ds(1, cells)], coarse_out.at[0], local_sem.at[0])
+    new_field.start()
     for s in range(0, 16, 4):
         stage4(s, 4)
 
@@ -329,16 +332,14 @@
     sent = []
 
     def finish(c, values):
-        q[c] = values.reshape(2, 32, 1024)
+        fine_out[c] = values.reshape(2, 32, 1024)
         hi, lo = halves(values)
         flat = mm(hi, mw[...]) + mm(lo, mw[...])
         hi, lo = halves(flat)
         means[c] = mm(pair, hi) + mm(pair, lo)
         back = remote(means.at[c], means_in.at[c], 5 + c, left)
         back.start()
-        store = pltpu.make_async_copy(q.at[c], fine_out.at[c], local_sem.at[2 + c])
-        store.start()
-        sent.append((back, store))
+        sent.append(back)
 
     for step in range(2):
         r = 0.5 * step
@@ -360,7 +361,8 @@
     eye = (iota((8, 128), 1) >> 4) == iota((8, 128), 0)
     z_lane = iota((16, 16, 256), 2)
 
-    into = (nf.at[pl.ds(1, cells)], npm)
+    new_field.wait()
+    into = (coarse_out.at[0], coarse_out.at[1])
 
     def insert(ref, c, i, keep, y, z):
         values = ref[c, pl.ds(16 * i, 16)]
@@ -378,20 +380,13 @@
             rows = pl.ds(16 * half, 16)
             into[c][:, rows] = jnp.where(here, block, into[c][:, rows])
 
-    stores = []
     for c in range(2):
         for i in range(2):
             insert(means, c, i, *corner[i])
     for c in range(2):
-        sent[c][0].wait()
+        sent[c].wait()
         for i in range(2):
             insert(means_in, c, i, *corner[2 + i])
-        store = pltpu.make_async_copy(into[c], coarse_out.at[c], local_sem.at[c])
-        store.start()
-        stores.append(store)
-    for c in range(2):
-        sent[c][1].wait()
-        stores[c].wait()
 
 
 def shards(devices, state, fine_state, box_list, plan):
@@ -401,24 +396,24 @@
     def slab(layers):
         return pltpu.VMEM((layers, ny, nz), F32)
 
-    any_spec = pl.BlockSpec(memory_space=pl.ANY)
     hbm_spec = pl.BlockSpec(memory_space=pltpu.HBM)
 
     def body(*refs):
         kernel(devices, *refs)
 
+    vmem_spec = pl.BlockSpec(memory_space=pltpu.VMEM)
     return pl.pallas_call(
         body,
         out_shape=(
-            jax.ShapeDtypeStruct(state.shape, F32),
-            jax.ShapeDtypeStruct(fine_state.shape, F32),
+            pltpu.VMEM(state.shape, F32),
+            pltpu.VMEM(fine_state.shape, F32),
         ),
         in_specs=[hbm_spec, hbm_spec, hbm_spec, hbm_spec],
-        out_specs=(any_spec, any_spec),
+        out_specs=(vmem_spec, vmem_spec),
         scratch_shapes=[
             slab(cells + 10), slab(cells + 8),
             slab(cells + 8), slab(cells + 6), slab(cells + 4),
-            slab(cells + 6), slab(cells + 4), slab(cells + 2), slab(cells),
+            slab(cells + 6), slab(cells + 4), slab(cells + 2),
             pltpu.VMEM(fine_state.shape, F32),
             pltpu.VMEM((2, 48, 1024), F32),
             pltpu.VMEM((2, 64, 128), F32), pltpu.VMEM((64, 128), F32),
@@ -431,7 +426,7 @@
             pltpu.SemaphoreType.DMA((7,)),
         ],
         compiler_params=pltpu.CompilerParams(
-            collective_id=0, has_side_effects=True, vmem_limit_bytes=48 * 1024 * 1024
+            collective_id=0, has_side_effects=True, vmem_limit_bytes=VMEM_LIMIT
         ),
         cost_estimate=pl.CostEstimate(flops=10**9, bytes_accessed=3 * 2**20, transcendentals=0),
         name="refined_step",

time: 30.6 us -> 27.1 us (0.89)
  local copies, waits for them, and re-layouts: 5.36 us -> 1.77 us
    unnamed x10 -> x2, local copies, waits for them, and re-layouts: 5.36 us -> 1.77 us
where the time goes in v2:
time: 27.1 us; the launch traced here: 26.9 us
  Pallas kernels  24.5 us (90%)
  local copies, waits for them, and re-layouts  1.77 us (7%)
  between operations  0.64 us (2%)
    pallas_call x1, Pallas kernels, shards(): pl.pallas_call(body, out_shape=(pltpu.VMEM(state.shape, F32), pltpu.VMEM(...  24.5 us
    unnamed x2, local copies, waits for them, and re-layouts  1.77 us

profile of v2, /device:TPU:0, one launch (start us, length us, event | category | flops | bytes accessed | tf_op | source)
XLA Modules:
  0.0 26.9 jit_solution(11573447781254985106)
XLA Ops:
  0.6 24.5 %refined_step.1 = (f32[2,16,32,256]{3,2,1,0:T(8,128)S(1)}, f32[2,2,32,1024]{3,2,1,0:T(8,128)S(1)}) custom-call(f32[2,16,32,256]{3,2,1,0:T(8,128)} %refs_0_.1, f32[2,2,32,1024]{3,2,1,0:T(8,128)} %refs_1_.1, s32[3,32]{1,0:T(4,128)} %bitcast.1, s32[32]{0:T(128)} %refs_3_.1), custom_call_target="tpu_custom_call" | custom-call | flops 1000000000 | bytes 3145728 | tf_op jit(solution)/shard_map/refined_step/pallas_call | solution.py:405
  25.2 1.0 %copy.8 = f32[2,16,32,256]{3,2,1,0:T(8,128)} copy(f32[2,16,32,256]{3,2,1,0:T(8,128)S(1)} %get-tuple-element.2) | data formatting | bytes 2097152
  26.1 0.8 %copy.9 = f32[2,2,32,1024]{3,2,1,0:T(8,128)} copy(f32[2,2,32,1024]{3,2,1,0:T(8,128)S(1)} %get-tuple-element.3) | data formatting | bytes 1048576

commit v3 on v2

--- a/solution.py
+++ b/solution.py
@@ -168,7 +168,9 @@
     def stage1(start, n):
         slope = force(fe, -5, start, n)
         k1[pl.ds(start + 3, n)] = slope
-        f3[pl.ds(start + 3, n)] = f2[pl.ds(start + 4, n)] + 0.0625 * slope
+
+    def fill_f3(start, n):
+        f3[pl.ds(start + 3, n)] = f2[pl.ds(start + 4, n)] + 0.0625 * k1[pl.ds(start + 3, n)]
 
     def stage2(start, n):
         slope = force(f2, -4, start, n)
@@ -193,6 +195,7 @@
         fill_f2(s, 4)
     for s in range(2, 14, 4):
         stage1(s, 4)
+        fill_f3(s, 4)
         stage2(s, 4)
     stage3(4, 4)
     stage3(8, 4)
@@ -229,31 +232,19 @@
     first = inside(f)
     second = inside(f + (h / 2) * p)
 
-    for copy in halo:
-        copy.wait()
-    for s in (-4, 16):
-        fill_f2(s, 4)
-    for s in (-3, 14):
-        stage1(s, 5)
-    for s in (-2, 14):
-        stage2(s, 4)
-    for s in (-1, 12):
-        stage3(s, 5)
-
     lane = iota((1, 128), 1)
     group = ((lane >> 6) << 1) + ((lane >> 4) & 1)
     lane_y = pick(group, [c[1] for c in corner])
     lane_z = pick(group, [c[2] for c in corner]) + (lane & 15)
     k = iota((256, 128), 0)
     hit = jnp.where(k == lane_z, 1.0, 0.0)
-    raw = None
     rows8 = iota((8, 1), 0)
     row_box = rows8 >> 1
     row_y = pick(row_box, [c[1] for c in corner])
     row_z = pick(row_box, [c[2] for c in corner])
     row_z = jnp.where((rows8 & 1) == 0, row_z + 255, row_z + 16) & 255
     side_hit = jnp.where(iota((8, 256), 1) == row_z, 1.0, 0.0).astype(BF)
-    for t, (ref, base) in enumerate(((fe, 4), (nf, 0))):
+    def extract(t, ref, base):
         body = ref[pl.ds(base + 1, cells)]
         rows = jnp.concatenate(
             [ref[base], ref[base + cells + 1], body[:, 31], body[:, 15], body[:, 16], body[:, 0]], axis=0
@@ -261,7 +252,6 @@
         hi, lo = halves(rows)
         weight = jnp.where(((iota((256, 128), 1) >> 5) & 1) == t, hit, 0.0).astype(BF)
         part = mm(hi, weight) + mm(lo, weight)
-        raw = part if raw is None else raw + part
         hi, lo = halves(body.reshape(cells * 32, 256))
         side = mm_nt(side_hit, hi) + mm_nt(side_hit, lo)
         side = jnp.where(jnp.broadcast_to(row_y, (8, 512)) == 0, side, roll(side, -16, 1))
@@ -270,6 +260,25 @@
                 patches[dest, pl.ds(32 + 8 * tile + 4 * t, 4)] = side[
                     4 * dest : 4 * dest + 4, 128 * tile : 128 * tile + 128
                 ]
+        return part
+
+    for copy in halo[:2]:
+        copy.wait()
+    for s in (-3, 14):
+        stage1(s, 5)
+    raw = extract(0, fe, 4)
+    for copy in halo[2:]:
+        copy.wait()
+    for s in (-4, 16):
+        fill_f2(s, 4)
+    for s in (-3, 14):
+        fill_f3(s, 5)
+    for s in (-2, 14):
+        stage2(s, 4)
+    for s in (-1, 12):
+        stage3(s, 5)
+
+    raw += extract(1, nf, 0)
     low = jnp.broadcast_to(lane_y, (16, 128)) == 0
     x_part = jnp.concatenate(
         [jnp.where(low, raw[0:16], raw[16:32]), jnp.where(low, raw[32:48], raw[48:64])], axis=0

time: 27.1 us -> 26.6 us (0.982)
  Pallas kernels: 24.5 us -> 24 us
    pallas_call x1, Pallas kernels: 24.5 us -> 24 us  [shards(): pl.pallas_call(body, out_shape=(pltpu.VMEM(state.shape, F32), pltpu.VMEM(...]
where the time goes in v3:
time: 26.6 us; the launch traced here: 26.4 us
  Pallas kernels  24 us (90%)
  local copies, waits for them, and re-layouts  1.77 us (7%)
  between operations  0.64 us (2%)
    pallas_call x1, Pallas kernels, shards(): pl.pallas_call(body, out_shape=(pltpu.VMEM(state.shape, F32), pltpu.VMEM(...  24 us
    unnamed x2, local copies, waits for them, and re-layouts  1.77 us

profile of v3, /device:TPU:0, one launch (start us, length us, event | category | flops | bytes accessed | tf_op | source)
XLA Modules:
  0.0 26.4 jit_solution(9769398824516458264)
XLA Ops:
  0.6 24.0 %refined_step.1 = (f32[2,16,32,256]{3,2,1,0:T(8,128)S(1)}, f32[2,2,32,1024]{3,2,1,0:T(8,128)S(1)}) custom-call(f32[2,16,32,256]{3,2,1,0:T(8,128)} %refs_0_.1, f32[2,2,32,1024]{3,2,1,0:T(8,128)} %refs_1_.1, s32[3,32]{1,0:T(4,128)} %bitcast.1, s32[32]{0:T(128)} %refs_3_.1), custom_call_target="tpu_custom_call" | custom-call | flops 1000000000 | bytes 3145728 | tf_op jit(solution)/shard_map/refined_step/pallas_call | solution.py:414
  24.7 1.0 %copy.8 = f32[2,16,32,256]{3,2,1,0:T(8,128)} copy(f32[2,16,32,256]{3,2,1,0:T(8,128)S(1)} %get-tuple-element.2) | data formatting | bytes 2097152
  25.6 0.8 %copy.9 = f32[2,2,32,1024]{3,2,1,0:T(8,128)} copy(f32[2,2,32,1024]{3,2,1,0:T(8,128)S(1)} %get-tuple-element.3) | data formatting | bytes 1048576
